TPU v7x, 128 devices: a whole 4x4x4 slice. The times are simulated.
128 devices in a mesh: ctx: 4 (over x_hi, core), wt: 32 (over z, x_lo, y).
Axes of the slice: x: 4 (x_hi: 2, x_lo: 2; x = x_hi * 2 + x_lo), y: 4, z: 4, core: 2. Of those that a mesh axis runs over, the one named last changes fastest.
Arguments:
- context_x: bfloat16 [4096, 8192], P('ctx'), may hold values from -16 to 16
- query_x: bfloat16 [1024, 8192], P(('ctx', 'wt')), may hold values from -16 to 16
- w_query: bfloat16 [8192, 4096], P('wt'), may hold values from -0.0625 to 0.0625
- key_value_weight: bfloat16 [8192, 1024], P('wt'), may hold values from -0.0625 to 0.0625
Outputs:
- context_out: bfloat16 [4096, 4096], P('ctx', 'wt')
- query_out: bfloat16 [1024, 4096], P('ctx', 'wt')
All inputs are finite; a program needn't handle non-finite values.
Results may differ from a plain program's by a relative error of at most 0.018.
The roundings to bfloat16 on the way count: a program that leaves them out, or rounds other values in their place, can miss the bound.
Values may be sent and summed in bfloat16 or wider, within the bound.
A program may use at most 128 MiB of HBM per device.

v0:
```python
import math

import jax
import jax.numpy as jnp
from jax import lax
from jax.sharding import PartitionSpec as P

HEAD_SIZE = 128
HQ = 32
GROUP = 8


rope_base = 500000.0


def spread(block, axis, owner):
    block = jnp.where(lax.axis_index(axis) == owner, block, jnp.zeros_like(block))
    return lax.psum(block, axis)


def joined(part, axis, combine):
    gathered = jax.tree.map(lambda a: lax.all_gather(a, axis), part)

    def take(source):
        return jax.tree.map(lambda a: lax.dynamic_index_in_dim(a, source, 0, False), gathered)

    return lax.fori_loop(
        1, lax.axis_size(axis), lambda source, state: combine(state, take(source)), take(0)
    )


def apply_rotation(projected, token_positions):
    token_rows = projected.shape[0]
    heads = projected.shape[1] // HEAD_SIZE
    half = HEAD_SIZE // 2
    shaped = projected.reshape(token_rows, heads, HEAD_SIZE)
    frequency = jnp.exp(
        -math.log(rope_base) * (2.0 * jnp.arange(half, dtype=jnp.float32) / HEAD_SIZE)
    )
    angle = token_positions.astype(jnp.float32)[:, None] * frequency[None, :]
    cosine = jnp.cos(angle)[:, None, :]
    sine_part = jnp.sin(angle)[:, None, :]
    lower_half = shaped[:, :, :half]
    upper_half = shaped[:, :, half:]
    turned = jnp.concatenate(
        [
            lower_half * cosine - upper_half * sine_part,
            upper_half * cosine + lower_half * sine_part,
        ],
        axis=2,
    )
    return turned.reshape(token_rows, heads * HEAD_SIZE)


def join_partial(first_part, second_part):
    top = jnp.maximum(first_part[0], second_part[0])
    first_factor = jnp.exp(first_part[0] - top)
    second_factor = jnp.exp(second_part[0] - top)
    mass = first_part[1] * first_factor + second_part[1] * second_factor
    values = first_part[2] * first_factor[:, :, None] + second_part[2] * second_factor[:, :, None]
    return (top, mass, values)


def per_device(context_x, query_x, w_query, key_value_weight):
    n_ctx = lax.axis_size("ctx")
    n_wt = lax.axis_size("wt")
    ctx_index = lax.axis_index("ctx")
    wt_index = lax.axis_index("wt")
    block = context_x.shape[0]
    heads_here = HQ // n_wt
    scale = 1.0 / math.sqrt(HEAD_SIZE)
    query_cols = lax.all_to_all(w_query, "wt", split_axis=1, concat_axis=0, tiled=True)
    every_pair = lax.all_gather(key_value_weight, "wt", axis=0, tiled=True)
    group = wt_index * heads_here // GROUP
    pair_cols = lax.dynamic_slice_in_dim(every_pair, group * 2 * HEAD_SIZE, 2 * HEAD_SIZE, 1)
    token_positions = ctx_index * block + jnp.arange(block, dtype=jnp.int32)
    own_q = apply_rotation(
        jnp.dot(context_x, query_cols, preferred_element_type=jnp.float32), token_positions
    ).astype(jnp.bfloat16)
    pair_proj = jnp.dot(context_x, pair_cols, preferred_element_type=jnp.float32)
    own_k = apply_rotation(pair_proj[:, :HEAD_SIZE], token_positions).astype(jnp.bfloat16)
    own_v = pair_proj[:, HEAD_SIZE:].astype(jnp.bfloat16)
    anchor = spread(jnp.stack([own_k, own_v]), "ctx", 0)
    q_shaped = own_q.reshape(block, heads_here, HEAD_SIZE)
    s_anchor = (
        jnp.einsum("qhd,kd->hqk", q_shaped, anchor[0], preferred_element_type=jnp.float32) * scale
    )
    s_anchor = jnp.where(ctx_index > 0, s_anchor, -1e30)
    causal = jnp.arange(block)[:, None] >= jnp.arange(block)[None, :]
    s_own = jnp.einsum("qhd,kd->hqk", q_shaped, own_k, preferred_element_type=jnp.float32) * scale
    s_own = jnp.where(causal[None], s_own, -1e30)
    top = jnp.maximum(jnp.max(s_anchor, axis=2), jnp.max(s_own, axis=2))
    p_anchor = jnp.exp(s_anchor - top[:, :, None])
    p_own = jnp.exp(s_own - top[:, :, None])
    total = jnp.sum(p_anchor, axis=2) + jnp.sum(p_own, axis=2)
    summed = jnp.einsum(
        "hqk,kd->qhd", p_anchor.astype(jnp.bfloat16), anchor[1], preferred_element_type=jnp.float32
    )
    summed = summed + jnp.einsum(
        "hqk,kd->qhd", p_own.astype(jnp.bfloat16), own_v, preferred_element_type=jnp.float32
    )
    context_out = (
        (summed / jnp.transpose(total)[:, :, None])
        .reshape(block, heads_here * HEAD_SIZE)
        .astype(jnp.bfloat16)
    )
    n_tokens = n_ctx * block
    piece = lax.all_gather(query_x, ("ctx", "wt"), axis=0, tiled=True)
    token_rows = piece.shape[0]
    query_pos = n_tokens + 0 + jnp.int32(0) + jnp.arange(token_rows, dtype=jnp.int32)
    q_part = apply_rotation(
        jnp.dot(piece, query_cols, preferred_element_type=jnp.float32), query_pos
    ).astype(jnp.bfloat16)
    kv_part = jnp.dot(piece, pair_cols, preferred_element_type=jnp.float32)
    k_part = apply_rotation(kv_part[:, :HEAD_SIZE], query_pos).astype(jnp.bfloat16)
    v_part = kv_part[:, HEAD_SIZE:].astype(jnp.bfloat16)
    projected = jnp.concatenate([q_part, k_part, v_part], axis=1)
    total_rows = projected.shape[0]
    q_all = projected[:, : heads_here * HEAD_SIZE].reshape(total_rows, heads_here, HEAD_SIZE)
    q_keys = projected[:, heads_here * HEAD_SIZE : (heads_here + 1) * HEAD_SIZE]
    q_vals = projected[:, (heads_here + 1) * HEAD_SIZE :]
    rows_here = total_rows // n_ctx
    row_start = ctx_index * rows_here
    s_context = jnp.einsum("qhd,kd->hqk", q_all, own_k, preferred_element_type=jnp.float32) * scale
    local_top = jnp.max(s_context, axis=2)
    weights = jnp.exp(s_context - local_top[:, :, None])
    mass = jnp.sum(weights, axis=2)
    value_sum = jnp.einsum(
        "hqk,kd->hqd", weights.astype(jnp.bfloat16), own_v, preferred_element_type=jnp.float32
    )
    merged = joined((local_top, mass, value_sum), "ctx", join_partial)
    top_here = lax.dynamic_slice_in_dim(merged[0], row_start, rows_here, 1)
    mass_here = lax.dynamic_slice_in_dim(merged[1], row_start, rows_here, 1)
    value_here = lax.dynamic_slice_in_dim(merged[2], row_start, rows_here, 1)
    q_here = lax.dynamic_slice_in_dim(q_all, row_start, rows_here, 0)
    s_self = jnp.einsum("qhd,kd->hqk", q_here, q_keys, preferred_element_type=jnp.float32) * scale
    self_causal = (row_start + jnp.arange(rows_here, dtype=jnp.int32))[:, None] >= jnp.arange(
        total_rows, dtype=jnp.int32
    )[None, :]
    s_self = jnp.where(self_causal[None], s_self, -1e30)
    top_all = jnp.maximum(top_here, jnp.max(s_self, axis=2))
    w_self = jnp.exp(s_self - top_all[:, :, None])
    shrink = jnp.exp(top_here - top_all)
    mass_all = mass_here * shrink + jnp.sum(w_self, axis=2)
    value_all = value_here * shrink[:, :, None] + jnp.einsum(
        "hqk,kd->hqd", w_self.astype(jnp.bfloat16), q_vals, preferred_element_type=jnp.float32
    )
    query_out = (
        jnp.transpose(value_all / mass_all[:, :, None], (1, 0, 2))
        .reshape(rows_here, heads_here * HEAD_SIZE)
        .astype(jnp.bfloat16)
    )
    return (context_out, query_out)


def solution(mesh):
    placed = (P("ctx", None), P(("ctx", "wt"), None), P("wt", None), P("wt", None))
    return jax.shard_map(
        per_device,
        mesh=mesh,
        in_specs=placed,
        out_specs=(P("ctx", "wt"), P("ctx", "wt")),
        check_vma=False,
    )
```

profile of v0, /device:TPU:1, one launch (start us, length us, event | category | flops | bytes accessed | tf_op | source)
XLA Modules:
  0.0 647.1 jit_solution(9619341534581976500)
XLA Ops:
  8.6 4.1 copy.14
  12.8 9.8 %all-to-all-start = ((bf16[256,32,128]{0,2,1:T(8,128)(2,1)}), bf16[256,32,128]{0,2,1:T(8,128)(2,1)S(1)}, u32[]{:S(2)}, u32[]{:S(2)}) async-start(bf16[256,32,128]{0,2,1:T(8,128)(2,1)} %bitcast.200), calls=%async_computation | async-start | bytes 4194304 | tf_op jit(solution)/shard_map/all_to_all | solution.py:72
  22.7 48.5 %all-to-all-done = bf16[256,32,128]{0,2,1:T(8,128)(2,1)S(1)} async-done(((bf16[256,32,128]{0,2,1:T(8,128)(2,1)}), bf16[256,32,128]{0,2,1:T(8,128)(2,1)S(1)}, u32[]{:S(2)}, u32[]{:S(2)}) %all-to-all-start) | async-done | bytes 2097184 | tf_op jit(solution)/shard_map/all_to_all | solution.py:72
  71.1 1.3 copy-done.1
  72.5 3.2 copy.15
  75.7 11.6 %convolution_bitcast_fusion.1 = f32[1024,1,128]{0,2,1:T(8,128)S(1)} fusion(bf16[1024,8192]{1,0:T(8,128)(2,1)} %param.6, bf16[8192,128]{1,0:T(8,128)(2,1)S(1)} %bitcast.197), kind=kOutput, calls=%fused_computation.44 | convolution fusion | flops 2147483648 | bytes 19398656 | tf_op jit(solution)/shard_map/dot_general | solution.py:78
  87.3 140.7 %all-gather.7.cloned.1.call-done = bf16[8192,1024]{1,0:T(8,128)(2,1)} async-done(((bf16[256,1024]{1,0:T(8,128)(2,1)}), bf16[8192,1024]{1,0:T(8,128)(2,1)}) %all-gather.7.cloned.1.call-update) | async-done | bytes 16777232 | tf_op jit(solution)/shard_map/all_gather | solution.py:73
  227.9 12.6 %fusion.29 = f32[1024,256]{0,1:T(8,128)} fusion(bf16[1024,8192]{1,0:T(8,128)(2,1)} %param.6, bf16[8192,1024]{1,0:T(8,128)(2,1)} %all-gather.7.cloned.1.call-done, s32[]{:T(128)S(6)} %select_n.61), kind=kOutput, calls=%fused_computation.38 | convolution fusion | flops 4294967296 | bytes 22020100 | tf_op jit(solution)/shard_map/dot_general | solution.py:80
  240.5 1.1 slice_bitcast_fusion.2
  241.6 1.2 fusion.77
  242.8 1.1 fusion.124
  243.9 0.9 maximum_select_fusion
  245.0 315.6 %all-gather.9.cloned.1.call-done = bf16[1024,8192]{1,0:T(8,128)(2,1)} async-done(((bf16[8,8192]{1,0:T(8,128)(2,1)}), bf16[1024,8192]{1,0:T(8,128)(2,1)}) %all-gather.9.cloned.1.call-update) | async-done | bytes 16777232 | tf_op jit(solution)/shard_map/all_gather | solution.py:108
  560.6 12.6 %fusion.32 = f32[1024,256]{0,1:T(8,128)} fusion(bf16[1024,8192]{1,0:T(8,128)(2,1)} %all-gather.9.cloned.1.call-done, bf16[8192,1024]{1,0:T(8,128)(2,1)} %all-gather.7.cloned.1.call-done, s32[]{:T(128)S(6)} %select_n.61), kind=kOutput, calls=%fused_computation.39 | convolution fusion | flops 4294967296 | bytes 22020100 | tf_op jit(solution)/shard_map/dot_general | solution.py:114
  573.2 1.9 slice_bitcast_fusion
  575.1 11.5 %convolution_bitcast_fusion = f32[1024,1,128]{0,2,1:T(8,128)S(1)} fusion(bf16[1024,8192]{1,0:T(8,128)(2,1)} %all-gather.9.cloned.1.call-done, bf16[8192,128]{1,0:T(8,128)(2,1)S(1)} %bitcast.198), kind=kOutput, calls=%fused_computation.43 | convolution fusion | flops 2147483648 | bytes 19398656 | tf_op jit(solution)/shard_map/dot_general | solution.py:112
  586.6 3.6 fusion.86
  591.0 1.9 copy-done
  592.9 1.7 fusion.19
  594.6 6.3 all-gather
  600.9 2.9 fusion.13
  603.9 6.9 %all-gather.1 = f32[4096]{0:T(1024)S(1)} all-gather(f32[1024]{0:T(1024)S(1)} %fusion.13), channel_id=3, replica_groups=mesh['ctx'=4,'wt'=32] {'ctx'}, dimensions={0}, use_global_device_ids=true | all-gather | bytes 20480 | tf_op jit(solution)/shard_map/all_gather | solution.py:22
  610.8 2.7 fusion.16
  613.4 1.8 fusion.5
  616.7 1.1 fusion.24
  619.7 13.7 %all-gather.11.cloned.1.call-done = f32[4096,128]{1,0:T(8,128)} async-done(((f32[1024,128]{1,0:T(8,128)}), f32[4096,128]{1,0:T(8,128)}) %all-gather.11.cloned.1.call-update) | async-done | bytes 2097168 | tf_op jit(solution)/shard_map/all_gather | solution.py:22
  633.4 1.1 slice_bitcast_fusion.1
  634.5 4.8 while.19
  634.6 1.6 fusion.137
  636.2 1.5 fusion.137
  637.8 1.5 fusion.137
  639.6 1.0 fusion.46
  (39 shorter events, 6.2 us)
Async XLA Ops:
  7.2 220.8 %all-gather.7.cloned.1.call-start = ((), (), s32[]{:S(2)}) async-start(), calls=%async_computation.1 | async-start | bytes 17301504 | tf_op jit(solution)/shard_map/all_gather | solution.py:73
  7.9 552.7 %all-gather.9.cloned.1.call-start = ((), (), s32[]{:S(2)}) async-start(), calls=%async_computation.3 | async-start | bytes 16908288 | tf_op jit(solution)/shard_map/all_gather | solution.py:108
  12.8 58.4 %all-to-all-start = ((bf16[256,32,128]{0,2,1:T(8,128)(2,1)}), bf16[256,32,128]{0,2,1:T(8,128)(2,1)S(1)}, u32[]{:S(2)}, u32[]{:S(2)}) async-start(bf16[256,32,128]{0,2,1:T(8,128)(2,1)} %bitcast.200), calls=%async_computation | async-start | bytes 4194304 | tf_op jit(solution)/shard_map/all_to_all | solution.py:72
  22.6 590.9 %all-reduce.2.cloned.1.call-start = ((), (), s32[]{:S(2)}) async-start(), calls=%async_computation.2 | async-start | bytes 1048576 | tf_op jit(solution)/shard_map/psum | solution.py:18
  71.1 1.3 copy-start.1
  244.8 388.7 %all-gather.11.cloned.1.call-start = ((), (), s32[]{:S(2)}) async-start(), calls=%async_computation.4 | async-start | bytes 2621440 | tf_op jit(solution)/shard_map/all_gather | solution.py:22
  586.6 6.3 copy-start.3
  591.0 1.9 copy-start
  613.4 2.7 copy-start.2
  615.3 1.4 copy-start.5
  634.5 5.0 copy-start.4
Sparse Core Ops, SparseCore 0:
  9.6 218.2 all-gather.6
  229.6 330.9 all-gather.8
  563.1 42.7 all-reduce.1
  607.4 25.9 all-gather.10
where the time goes:
time: 648 us; the launch traced here: 647 us
  waiting for transfers between devices  520 us (80%)
  matrix products  58.4 us (9%)
  local copies, waits for them, and re-layouts  16.5 us (3%)
  other arithmetic  14.9 us (2%)
  between operations  14 us (2%)
  blocking collectives  13.2 us (2%)
  starting transfers between devices  10.2 us (2%)
    all_gather x1, waiting for transfers between devices, per_device(): piece = lax.all_gather(query_x, ('ctx', 'wt'), axis=0, tiled=True)  316 us
    all_gather x1, waiting for transfers between devices, per_device(): every_pair = lax.all_gather(key_value_weight, 'wt', axis=0, tiled=True)  141 us
    all_to_all x1, waiting for transfers between devices, per_device(): lax.all_to_all(w_query, 'wt', split_axis=1, concat_axis=0, tiled=True)  48.5 us
    all_gather x1, waiting for transfers between devices, joined(): gathered = jax.tree.map(lambda a: lax.all_gather(a, axis), part)  13.7 us
    all_gather x2, blocking collectives, joined(): gathered = jax.tree.map(lambda a: lax.all_gather(a, axis), part)  13.2 us
  transfers between devices with their start and end apart: 5, of which 4 were waited for; matrix products, arithmetic and copies ran while one was open for 12% of the time, Pallas kernels for 0%

commit v1 on v0

v1 whole, which is shorter than its diff:
```python
import math

import jax
import jax.numpy as jnp
import numpy as np
from jax import lax
from jax.experimental import pallas as pl
from jax.experimental.pallas import tpu as pltpu
from jax.sharding import PartitionSpec as P


BF = jnp.bfloat16
F32 = jnp.float32
D = 128
NS, NY = 8, 4
CTX_ROWS = 1024
Q_ROWS = 256
TOKENS = 4096
POSITIONS = 5120
EXP2_SCALE = math.log2(math.e) / math.sqrt(D)
MESH = pl.DeviceIdType.MESH
VMEM_LIMIT = 56 * 1024 * 1024


def rope_tables():
    half = D // 2
    frequency = 500000.0 ** (-2.0 * np.arange(half) / D)
    angle = np.arange(POSITIONS)[:, None] * frequency[None, :]
    cos, sin = np.cos(angle), np.sin(angle)
    by_row = np.stack([np.concatenate([cos, cos], 1), np.concatenate([-sin, sin], 1)])
    cos_t = np.concatenate([cos.T.reshape(4, 16, POSITIONS), np.ones((1, 16, POSITIONS))])
    sin_t = np.concatenate([sin.T.reshape(4, 16, POSITIONS), np.zeros((1, 16, POSITIONS))])
    return by_row.astype(np.float32), np.stack([cos_t, sin_t]).astype(np.float32)


def nt_dot(a, b):
    return lax.dot_general(a, b, (((1,), (1,)), ((), ())), preferred_element_type=F32)


SENDS = dict(kv1=8, w1=8, a1=4, a2=8, kvt_p=1, kw2=4, kw2_p=1, w1_p=8, w2=32, w2_p=8, c=4,
             kc_y=4, kc_x=4, kc_p=4, kq_y=4, kq_x=4, kq_p=4)
BASE = {}
_n = 0
for _name, _count in SENDS.items():
    BASE[_name] = _n
    _n += _count
SLOTS = _n


def project_kernel(x_hbm, qx, wq_hbm, kvw_hbm, tabq_hbm, tabk_hbm,
                   cq_out, qq_out, kvc_out, kvq_out,
                   x_v, w1, kv1, kv1t, w2, kw2t, kws, asend, a1, a_all, ar, kq, csend, crecv,
                   kvc, kvq, ut, tab_c, tab_q, tab_kc, tab_kq,
                   send_sem, recv_sem, x_sem, tab_sem, out_sem):
    ctx = lax.axis_index("ctx")
    wt = lax.axis_index("wt")
    x_hi, core = ctx // 2, lax.rem(ctx, 2)
    z, x_lo, y = wt // 8, lax.rem(wt // 4, 2), lax.rem(wt, 4)
    s_me = z * 2 + x_lo
    j_me = x_lo * 4 + y
    x_me = x_hi * 2 + x_lo
    partner = (x_hi * 2 + 1 - core, wt)

    def y_at(k):
        return lax.rem(y + k, 4)

    def y_dev(k):
        return (ctx, s_me * 4 + y_at(k))

    def s_at(k):
        z2 = lax.rem(z + k // 2, 4)
        x2 = x_lo if k % 2 == 0 else 1 - x_lo
        return z2 * 2 + x2

    def s_dev(k):
        return (ctx, s_at(k) * 4 + y)

    def x_at(k):
        return lax.rem(x_me + k, 4)

    def x_dev(k):
        x2 = x_at(k)
        return ((x2 // 2) * 2 + core, z * 8 + lax.rem(x2, 2) * 4 + y)

    def rcopy(name, src, dst, slot_send, slot_recv, dev):
        return pltpu.make_async_remote_copy(
            src_ref=src, dst_ref=dst, send_sem=send_sem.at[BASE[name] + slot_send],
            recv_sem=recv_sem.at[BASE[name] + slot_recv], device_id=dev, device_id_type=MESH)

    started = []

    def send(name, src, dst, slot_send, slot_recv, dev):
        copy = rcopy(name, src, dst, slot_send, slot_recv, dev)
        copy.start()
        started.append(copy)

    def arrived(name, dst, slot):
        rcopy(name, dst, dst, 0, slot, partner).wait_recv()

    tabs = [
        pltpu.make_async_copy(tabq_hbm.at[:, pl.ds(pl.multiple_of(ctx * 1024, 1024), 1024)], tab_c, tab_sem.at[0]),
        pltpu.make_async_copy(tabq_hbm.at[:, pl.ds(pl.multiple_of(TOKENS + ctx * 256, 256), 256)], tab_q, tab_sem.at[1]),
        pltpu.make_async_copy(tabk_hbm.at[:, jnp.minimum(j_me, 4), :, pl.ds(pl.multiple_of(ctx * 1024, 1024), 1024)], tab_kc, tab_sem.at[2]),
        pltpu.make_async_copy(tabk_hbm.at[:, jnp.minimum(j_me, 4), :, pl.ds(pl.multiple_of(TOKENS + ctx * 256, 256), 256)], tab_kq, tab_sem.at[3]),
    ]
    x_loads = [
        pltpu.make_async_copy(x_hbm.at[:, pl.ds(s * 1024, 1024)], x_v.at[s], x_sem.at[s])
        for s in range(NS)
    ]
    half_rows = pl.ds(pl.multiple_of(core * 128, 128), 128)

    def kv_cols(s):
        return pl.ds(pl.multiple_of(s * 128, 128), 128)

    def q_cols(s):
        return pl.ds(pl.multiple_of(s * 512, 512), 512)

    own_kv = pltpu.make_async_copy(kvw_hbm.at[half_rows, kv_cols(s_me)], kv1.at[s_me], recv_sem.at[BASE["kv1"] + s_me])
    own_kv.start()
    own_w = pltpu.make_async_copy(wq_hbm.at[half_rows, q_cols(s_me)], w1.at[s_me, core], recv_sem.at[BASE["w1"] + s_me])
    own_w.start()

    barrier = pltpu.get_barrier_semaphore()
    peers = [partner] + [y_dev(k) for k in range(1, 4)] + [s_dev(k) for k in range(1, 8)]
    peers += [((1 - x_hi) * 2 + core, s_me * 4 + y),
              ((1 - x_hi) * 2 + core, (z * 2 + 1 - x_lo) * 4 + y)]
    for dev in peers:
        pl.semaphore_signal(barrier, inc=1, device_id=dev, device_id_type=MESH)

    f = qx[...].astype(F32)
    for yy in range(NY):
        for s in range(NS):
            at = s * 1024 + yy * 256
            tile = jnp.concatenate([f[:, at:at + 128], f[:, at + 128:at + 256]], axis=0)
            asend[yy, s * 16:(s + 1) * 16, :] = tile.astype(BF)
    a1[y] = asend[y]
    pl.semaphore_wait(barrier, len(peers))

    for k in range(1, 8):
        send("kv1", kvw_hbm.at[half_rows, kv_cols(s_at(k))], kv1.at[s_me], k, s_me, s_dev(k))
    for k in range(1, 4):
        send("a1", asend.at[y_at(k)], a1.at[y], k, y, y_dev(k))
    for k in range(1, 8):
        send("w1", wq_hbm.at[half_rows, q_cols(s_at(k))], w1.at[s_me, core], k, s_me, s_dev(k))
    for copy in x_loads:
        copy.start()
    for copy in tabs:
        copy.start()

    own_kv.wait()
    for k in range(1, 8):
        arrived("kv1", kv1.at[s_at(k)], s_at(k))
    for s in range(NS):
        by_col = kv1[s].T
        pairs = jnp.concatenate(
            [by_col[at + 16 * yy:at + 16 * yy + 16] for yy in range(NY) for at in (0, 64)], axis=0)
        kv1t[core, :, s * 128:(s + 1) * 128] = jnp.where(x_lo == 0, pairs, by_col)
    for k in range(1, 4):
        send("kw2", kv1t.at[core, pl.ds(pl.multiple_of(y_at(k) * 32, 32), 32)], kw2t.at[y, core], k, y, y_dev(k))
    send("kvt_p", kv1t.at[core], kv1t.at[core], 0, 0, partner)
    kw2t[y, core] = kv1t[core, pl.ds(pl.multiple_of(y * 32, 32), 32), :]

    for k in range(1, 4):
        arrived("a1", a1.at[y_at(k)], y_at(k))
    for k in range(1, 8):
        send("a2", a1, a_all.at[s_me], k, s_me, s_dev(k))
    a_all[s_me] = a1[...]

    for k in range(8):
        s = s_at(k)
        if k == 0:
            own_w.wait()
        else:
            arrived("w1", w1.at[s, core], s)
        for m in range(1, 4):
            send("w2", w1.at[s, core, :, pl.ds(pl.multiple_of(y_at(m) * 128, 128), 128)],
                 w2.at[s, y, core], k * 4 + m, s * 4 + y, y_dev(m))
        send("w1_p", w1.at[s, core], w1.at[s, core], k, s, partner)
        w2[s, y, core] = w1[s, core, :, pl.ds(pl.multiple_of(y * 128, 128), 128)]

    for k in range(1, 4):
        arrived("kw2", kw2t.at[y_at(k), core], y_at(k))
    send("kw2_p", kw2t.at[:, core], kw2t.at[:, core], 0, 0, partner)
    arrived("kw2_p", kw2t.at[:, 1 - core], 0)

    for s in range(NS):
        for yy in range(NY):
            for h in range(2):
                at = yy * 256 + h * 128
                kws[s, :, at:at + 128] = kw2t[yy, h, :, s * 128:(s + 1) * 128]
    for copy in x_loads:
        copy.wait()
    for copy in tabs:
        copy.wait()

    @pl.loop(0, 4)
    def _(m):
        rows = pl.ds(pl.multiple_of(m * 256, 256), 256)
        total = nt_dot(x_v[0, rows, :], kws[0])
        for s in range(1, NS):
            total = total + nt_dot(x_v[s, rows, :], kws[s])
        ut[:, rows] = total.T

    low, high = ut[0:16, :], ut[16:32, :]
    cos, sin = tab_kc[0], tab_kc[1]
    kvc[ctx, j_me, 0:16, :] = (low * cos - high * sin).astype(BF)
    kvc[ctx, j_me, 16:32, :] = (high * cos + low * sin).astype(BF)
    for k in range(1, 4):
        send("kc_y", kvc.at[ctx, j_me], kvc.at[ctx, j_me], k, y, y_dev(k))

    for k in range(1, 8):
        arrived("a2", a_all.at[s_at(k)], s_at(k))
    for t in range(NS):
        v = a_all[:, :, t * 16:(t + 1) * 16, :].astype(F32).reshape(32, 2, 8, 128)
        ar[:, t * 256:t * 256 + 128] = v[:, 0].reshape(256, 128).astype(BF)
        ar[:, t * 256 + 128:(t + 1) * 256] = v[:, 1].reshape(256, 128).astype(BF)
    arrived("kvt_p", kv1t.at[1 - core], 0)
    for s in range(NS):
        for h in range(2):
            at = s * 256 + h * 128
            kq[:, at:at + 128] = kv1t[h, :, s * 128:(s + 1) * 128]
    for s in range(NS):
        arrived("w1_p", w1.at[s, 1 - core], s)
    kv_part = nt_dot(ar[...], kq[...]).T
    for yy in range(NY):
        csend[yy, 256:288, :] = kv_part[yy * 32:(yy + 1) * 32, 0:128]
        csend[yy, 288:320, :] = kv_part[yy * 32:(yy + 1) * 32, 128:256]

    @pl.loop(0, 2)
    def _(m):
        rows = pl.ds(pl.multiple_of(m * 128, 128), 128)
        part = jnp.dot(ar[rows, :], w1[...].reshape(2048, 512), preferred_element_type=F32)
        for yy in range(NY):
            csend[yy, rows, :] = part[:, yy * 128:(yy + 1) * 128]

    for k in range(1, 4):
        send("c", csend.at[y_at(k)], crecv.at[y], k, y, y_dev(k))
    crecv[y] = csend[y]

    def kv_hop_x(name, buf):
        for k in range(1, 4):
            block = buf.at[ctx, x_lo * 4 + y_at(k)]
            arrived(name + "_y", block, y_at(k))
        mine = buf.at[ctx, pl.ds(x_lo * 4, 4)]
        for k in range(1, 4):
            send(name + "_x", mine, mine, k, x_me, x_dev(k))
        send(name + "_p", mine, mine, 0, x_me, partner)

    def of_x(buf, xs, cc):
        return buf.at[(xs // 2) * 2 + cc, pl.ds(lax.rem(xs, 2) * 4, 4)]

    def kv_hop_core(name, buf):
        for k in range(1, 4):
            block = of_x(buf, x_at(k), core)
            arrived(name + "_x", block, x_at(k))
            send(name + "_p", block, block, k, x_at(k), partner)

    def kv_last(name, buf):
        for k in range(4):
            arrived(name + "_p", of_x(buf, x_at(k), 1 - core), x_at(k))

    kv_hop_x("kc", kvc)

    for k in range(8):
        s = s_at(k)
        for m in range(1, 4):
            arrived("w2", w2.at[s, y_at(m), core], s * 4 + y_at(m))
        send("w2_p", w2.at[s, :, core], w2.at[s, :, core], k, s, partner)

    for k in range(1, 4):
        arrived("c", crecv.at[y_at(k)], y_at(k))
    total = crecv[0] + crecv[1] + crecv[2] + crecv[3]
    u = total[0:256]
    qq_out[...] = (u * tab_q[0] + pltpu.roll(u, 64, 1) * tab_q[1]).astype(BF)
    u = jnp.concatenate([total[256:288], total[288:320]], axis=1)
    low, high = u[0:16], u[16:32]
    cos, sin = tab_kq[0], tab_kq[1]
    kvq[ctx, j_me, 0:16, :] = (low * cos - high * sin).astype(BF)
    kvq[ctx, j_me, 16:32, :] = (high * cos + low * sin).astype(BF)
    for k in range(1, 4):
        send("kq_y", kvq.at[ctx, j_me], kvq.at[ctx, j_me], k, y, y_dev(k))

    kv_hop_core("kc", kvc)
    kv_hop_x("kq", kvq)

    for s in range(NS):
        arrived("w2_p", w2.at[s, :, 1 - core], s)

    @pl.loop(0, 4)
    def _(m):
        rows = pl.ds(pl.multiple_of(m * 256, 256), 256)
        total = jnp.dot(x_v[0, rows, :], w2[0].reshape(1024, D), preferred_element_type=F32)
        for s in range(1, NS):
            total = total + jnp.dot(x_v[s, rows, :], w2[s].reshape(1024, D), preferred_element_type=F32)
        cq_out[rows, :] = (total * tab_c[0, rows, :] + pltpu.roll(total, 64, 1) * tab_c[1, rows, :]).astype(BF)

    kv_hop_core("kq", kvq)
    kv_last("kc", kvc)
    out_c = pltpu.make_async_copy(kvc, kvc_out, out_sem.at[0])
    out_c.start()
    kv_last("kq", kvq)
    out_q = pltpu.make_async_copy(kvq, kvq_out, out_sem.at[1])
    out_q.start()
    for copy in started:
        copy.wait_send()
    out_c.wait()
    out_q.wait()


def project(context_x, query_x, w_query, key_value_weight, by_row, by_column):
    any_spec = pl.BlockSpec(memory_space=pl.ANY)
    vmem = pl.BlockSpec(memory_space=pltpu.VMEM)
    return pl.pallas_call(
        project_kernel,
        out_shape=[
            jax.ShapeDtypeStruct((CTX_ROWS, D), BF),
            jax.ShapeDtypeStruct((Q_ROWS, D), BF),
            jax.ShapeDtypeStruct((4, 8, 32, 1024), BF),
            jax.ShapeDtypeStruct((4, 8, 32, 256), BF),
        ],
        in_specs=[any_spec, vmem, any_spec, any_spec, any_spec, any_spec],
        out_specs=[vmem, vmem, any_spec, any_spec],
        scratch_shapes=[
            pltpu.VMEM((NS, CTX_ROWS, 1024), BF),
            pltpu.VMEM((NS, 2, 128, 512), BF),
            pltpu.VMEM((NS, 128, 128), BF),
            pltpu.VMEM((2, 128, 1024), BF),
            pltpu.VMEM((NS, NY, 2, 128, 128), BF),
            pltpu.VMEM((NY, 2, 32, 1024), BF),
            pltpu.VMEM((NS, 32, 1024), BF),
            pltpu.VMEM((NY, 128, 128), BF),
            pltpu.VMEM((NY, 128, 128), BF),
            pltpu.VMEM((NS, NY, 128, 128), BF),
            pltpu.VMEM((Q_ROWS, 2048), BF),
            pltpu.VMEM((128, 2048), BF),
            pltpu.VMEM((NY, 320, 128), F32),
            pltpu.VMEM((NY, 320, 128), F32),
            pltpu.VMEM((4, 8, 32, 1024), BF),
            pltpu.VMEM((4, 8, 32, 256), BF),
            pltpu.VMEM((32, 1024), F32),
            pltpu.VMEM((2, CTX_ROWS, D), F32),
            pltpu.VMEM((2, Q_ROWS, D), F32),
            pltpu.VMEM((2, 16, 1024), F32),
            pltpu.VMEM((2, 16, 256), F32),
            pltpu.SemaphoreType.DMA((SLOTS,)),
            pltpu.SemaphoreType.DMA((SLOTS,)),
            pltpu.SemaphoreType.DMA((NS,)),
            pltpu.SemaphoreType.DMA((4,)),
            pltpu.SemaphoreType.DMA((2,)),
        ],
        compiler_params=pltpu.CompilerParams(
            collective_id=0, has_side_effects=True, vmem_limit_bytes=VMEM_LIMIT),
        name="project",
    )(context_x, query_x, w_query, key_value_weight, by_row, by_column)


def weights_of(scores):
    top = jnp.max(scores[0], axis=1, keepdims=True)
    for s in scores[1:]:
        top = jnp.maximum(top, jnp.max(s, axis=1, keepdims=True))
    weights = [jnp.exp2((s - top) * EXP2_SCALE) for s in scores]
    total = jnp.sum(weights[0], axis=1, keepdims=True)
    for w in weights[1:]:
        total = total + jnp.sum(w, axis=1, keepdims=True)
    return [w.astype(BF) for w in weights], total


def attend_kernel(cq, qq, kvc, kvq, c_out, q_out, keys, values, qkeys, qvalues):
    ctx = lax.axis_index("ctx")
    for b in range(4):
        keys[b] = jnp.concatenate(
            [kvc[b, j, 0:16, :] for j in range(4)] + [kvc[b, j, 16:32, :] for j in range(4)], axis=0)
        values[b] = kvc[b, 4:8].reshape(128, 1024).T
        qkeys[:, b * 256:(b + 1) * 256] = jnp.concatenate(
            [kvq[b, j, 0:16, :] for j in range(4)] + [kvq[b, j, 16:32, :] for j in range(4)], axis=0)
        qvalues[b * 256:(b + 1) * 256, :] = kvq[b, 4:8].reshape(128, 256).T

    for i in range(4):
        q = cq[i * 256:(i + 1) * 256, :]
        wide = (i + 1) * 256
        s_anchor = jnp.dot(q, keys[0], preferred_element_type=F32)
        s_anchor = jnp.where(ctx > 0, s_anchor, -1e30)
        s_own = jnp.dot(q, keys[ctx, :, 0:wide], preferred_element_type=F32)
        row = lax.broadcasted_iota(jnp.int32, (256, wide), 0) + i * 256
        col = lax.broadcasted_iota(jnp.int32, (256, wide), 1)
        s_own = jnp.where(row >= col, s_own, -1e30)
        (p_anchor, p_own), total = weights_of([s_anchor, s_own])
        out = jnp.dot(p_anchor, values[0], preferred_element_type=F32)
        out = out + jnp.dot(p_own, values[ctx, 0:wide, :], preferred_element_type=F32)
        c_out[i * 256:(i + 1) * 256, :] = (out / total).astype(BF)

    for i in range(2):
        q = qq[i * 128:(i + 1) * 128, :]
        scores = [jnp.dot(q, keys[b], preferred_element_type=F32) for b in range(4)]
        s_self = jnp.dot(q, qkeys[...], preferred_element_type=F32)
        row = lax.broadcasted_iota(jnp.int32, (128, 1024), 0) + (ctx * 256 + i * 128)
        col = lax.broadcasted_iota(jnp.int32, (128, 1024), 1)
        scores.append(jnp.where(row >= col, s_self, -1e30))
        weights, total = weights_of(scores)
        out = jnp.dot(weights[4], qvalues[...], preferred_element_type=F32)
        for b in range(4):
            out = out + jnp.dot(weights[b], values[b], preferred_element_type=F32)
        q_out[i * 128:(i + 1) * 128, :] = (out / total).astype(BF)


def attend(cq, qq, kvc, kvq):
    vmem = pl.BlockSpec(memory_space=pltpu.VMEM)
    return pl.pallas_call(
        attend_kernel,
        out_shape=[jax.ShapeDtypeStruct((CTX_ROWS, D), BF), jax.ShapeDtypeStruct((Q_ROWS, D), BF)],
        in_specs=[vmem] * 4,
        out_specs=[vmem] * 2,
        scratch_shapes=[
            pltpu.VMEM((4, 128, 1024), BF),
            pltpu.VMEM((4, 1024, 128), BF),
            pltpu.VMEM((128, 1024), BF),
            pltpu.VMEM((1024, 128), BF),
        ],
        compiler_params=pltpu.CompilerParams(vmem_limit_bytes=VMEM_LIMIT),
        name="attend",
    )(cq, qq, kvc, kvq)


def per_device(context_x, query_x, w_query, key_value_weight):
    by_row, by_column = rope_tables()
    cq, qq, kvc, kvq = project(
        context_x, query_x, w_query, key_value_weight, jnp.asarray(by_row), jnp.asarray(by_column))
    return tuple(attend(cq, qq, kvc, kvq))


def solution(mesh):
    placed = (P("ctx", None), P(("ctx", "wt"), None), P("wt", None), P("wt", None))
    return jax.shard_map(
        per_device,
        mesh=mesh,
        in_specs=placed,
        out_specs=(P("ctx", "wt"), P("ctx", "wt")),
        check_vma=False,
    )
```

time: 648 us -> 70.8 us (0.11)
  waiting for transfers between devices: 520 us -> 0 us
  Pallas kernels: 0 us -> 70 us
  matrix products: 58.4 us -> 0 us
  local copies, waits for them, and re-layouts: 16.5 us -> 0 us
  other arithmetic: 14.9 us -> 0 us
  between operations: 14 us -> 0.64 us
  blocking collectives: 13.2 us -> 0 us
  starting transfers between devices: 10.2 us -> 0 us
    all_gather x3 -> x0, waiting for transfers between devices: 470 us -> none  [the longest x1 316 us: per_device(): piece = lax.all_gather(query_x, ('ctx', 'wt'), axis=0, tiled=True)]
    pallas_call x0 -> x2, Pallas kernels: none -> 70 us  [the longest x1 62 us: project(): pl.pallas_call(project_kernel, out_shape=[jax.ShapeDtypeStruct((CTX_ROWS,...]
    dot_general x12 -> x0, matrix products: 58.4 us -> none  [the longest x1 12.6 us: per_device(): jnp.dot(context_x, pair_cols, preferred_element_type=jnp.float32)]
    all_to_all x1 -> x0, waiting for transfers between devices: 48.5 us -> none  [per_device(): lax.all_to_all(w_query, 'wt', split_axis=1, concat_axis=0, tiled=True)]
    all_gather x2 -> x0, blocking collectives: 13.2 us -> none  [joined(): gathered = jax.tree.map(lambda a: lax.all_gather(a, axis), part)]
    all_to_all x1 -> x0, starting transfers between devices: 9.81 us -> none  [per_device(): lax.all_to_all(w_query, 'wt', split_axis=1, concat_axis=0, tiled=True)]
    unnamed x14 -> x0, local copies, waits for them, and re-layouts: 8.22 us -> none
  transfers between devices with their start and end apart: 5 -> 0, of which waited for: 4 -> 0; matrix products, arithmetic and copies ran while one was open for 12% -> 0% of each run, Pallas kernels for 0% -> 0%
where the time goes in v1:
time: 70.8 us; the launch traced here: 70.7 us
  Pallas kernels  70 us (99%)
    pallas_call x1, Pallas kernels, project(): pl.pallas_call(project_kernel, out_shape=[jax.ShapeDtypeStruct((CTX_ROWS,...  62 us
    pallas_call x1, Pallas kernels, attend(): pl.pallas_call(attend_kernel, out_shape=[jax.ShapeDtypeStruct((CTX_ROWS,...  8.04 us

profile of v1, /device:TPU:1, one launch (start us, length us, event | category | flops | bytes accessed | tf_op | source)
XLA Modules:
  0.0 70.7 jit_solution(7960555673842273216)
XLA Ops:
  0.6 62.0 %project.1 = (bf16[1024,128]{1,0:T(8,128)(2,1)}, bf16[256,128]{1,0:T(8,128)(2,1)}, bf16[4,8,32,1024]{3,2,1,0:T(8,128)(2,1)}, bf16[4,8,32,256]{3,2,1,0:T(8,128)(2,1)}) custom-call(bf16[1024,8192]{1,0:T(8,128)(2,1)} %x_hbm.1, bf16[8,8192]{1,0:T(8,128)(2,1)} %qx.1, bf16[256,4096]{1,0:T(8,128)(2,1)} %wq_hbm.1, bf16[256,1024]{1,0:T(8,128)(2,1)} %kvw_hbm.1, ...), custom_call_target="tpu_custom_call" | custom-call | tf_op jit(solution)/shard_map/project/pallas_call | solution.py:313
  62.6 8.0 %attend.1 = (bf16[1024,128]{1,0:T(8,128)(2,1)}, bf16[256,128]{1,0:T(8,128)(2,1)}) custom-call(bf16[1024,128]{1,0:T(8,128)(2,1)} %get-tuple-element.6.cq, bf16[256,128]{1,0:T(8,128)(2,1)} %get-tuple-element.7.qq, bf16[4,8,32,1024]{3,2,1,0:T(8,128)(2,1)} %get-tuple-element.8.kvc, bf16[4,8,32,256]{3,2,1,0:T(8,128)(2,1)} %get-tuple-element.9.kvq), custom_call_target="tpu_custom_call" | custom-call | tf_op jit(solution)/shard_map/attend/pallas_call | solution.py:408

commit v2 on v0

v2 whole, which is shorter than its diff:
```python
import math

import jax
import jax.numpy as jnp
import numpy as np
from jax import lax
from jax.experimental import pallas as pl
from jax.experimental.pallas import tpu as pltpu
from jax.sharding import PartitionSpec as P


BF = jnp.bfloat16
F32 = jnp.float32
D = 128
NS, NY = 8, 4
CTX_ROWS = 1024
Q_ROWS = 256
TOKENS = 4096
POSITIONS = 5120
EXP2_SCALE = math.log2(math.e) / math.sqrt(D)
MESH = pl.DeviceIdType.MESH
VMEM_LIMIT = 56 * 1024 * 1024


def rope_tables():
    half = D // 2
    frequency = 500000.0 ** (-2.0 * np.arange(half) / D)
    angle = np.arange(POSITIONS)[:, None] * frequency[None, :]
    cos, sin = np.cos(angle), np.sin(angle)
    by_row = np.stack([np.concatenate([cos, cos], 1), np.concatenate([-sin, sin], 1)])
    shape = (1, 4, 16, POSITIONS)
    cos_t = np.concatenate([cos.T.reshape(shape), np.ones(shape)])
    sin_t = np.concatenate([sin.T.reshape(shape), np.zeros(shape)])
    return by_row.astype(np.float32), np.stack([cos_t, sin_t]).astype(np.float32)


def nt_dot(a, b):
    return lax.dot_general(a, b, (((1,), (1,)), ((), ())), preferred_element_type=F32)


SLOTS_OF = dict(kvd=32, kvd_p=4, kv1=16, kv1_p=2, w1=16, a1=16, a2=8, w1_p=16, w2=64, w2_p=16, ck=8, cq=8,
                kc_y=4, kc_x=4, kc_p=4, kq_y=4, kq_x=4, kq_p=1)
BASE = {}
SLOTS = 0
for _name, _count in SLOTS_OF.items():
    BASE[_name] = SLOTS
    SLOTS += _count


def scores_of(q, keys):
    return jnp.dot(q, keys, preferred_element_type=F32)


def attend(scores, values, before=None):
    top = jnp.max(scores[0], axis=1, keepdims=True)
    for s in scores[1:]:
        top = jnp.maximum(top, jnp.max(s, axis=1, keepdims=True))
    if before is not None:
        top = jnp.maximum(top, before[0])
    total = out = None
    for s, v in zip(scores, values):
        w = jnp.exp2((s - top) * EXP2_SCALE)
        t = jnp.sum(w, axis=1, keepdims=True)
        o = jnp.dot(w.astype(BF), v, preferred_element_type=F32)
        total, out = (t, o) if total is None else (total + t, out + o)
    if before is not None:
        shrink = jnp.exp2((before[0] - top) * EXP2_SCALE)
        total = total + before[1] * shrink
        out = out + before[2] * shrink
    return top, total, out


def layer_kernel(x_hbm, qx, wq_hbm, kvw_hbm, tabq_hbm, tabk_hbm, c_out, q_out,
                 x_v, w_src, kv_src, kvt, kva, kws, w1, w2, asend, a1_0, a1_1, a_all, ar,
                 ck_send, ck_recv, cq_send, cq_recv,
                 kvc, kvq, acc, qq, keys, values, qkeys, qvalues, part_m, part_l, part_o,
                 tab_c, tab_q, tab_kc, tab_kq, send_sem, recv_sem, x_sem, tab_sem, load_sem):
    ctx = lax.axis_index("ctx")
    wt = lax.axis_index("wt")
    x_hi, core = ctx // 2, lax.rem(ctx, 2)
    z, x_lo, y = wt // 8, lax.rem(wt // 4, 2), lax.rem(wt, 4)
    x_me = x_hi * 2 + x_lo
    partner = (x_hi * 2 + 1 - core, wt)
    o_me, b_me = (z, y), (y, z)
    so_me = (z * 2 + x_lo, y * 2 + x_lo)

    def plus(a, k):
        return lax.rem(a + k, 4)

    def device(c, z2, x2, y2):
        return (c, z2 * 8 + x2 * 4 + y2)

    def x_side(k):
        return x_lo if k % 2 == 0 else 1 - x_lo

    def so_at(col, k):
        return plus(o_me[col], k // 2) * 2 + x_side(k)

    def so_dev(col, k):
        c2 = ctx if k % 2 == 0 else lax.rem(x_hi + core, 2) * 2 + core
        o2 = plus(o_me[col], k // 2)
        return device(c2, o2, x_side(k), y) if col == 0 else device(c2, z, x_side(k), o2)

    def b_dev(col, k):
        return device(ctx, z, x_lo, plus(y, k)) if col == 0 else device(ctx, plus(z, k), x_lo, y)

    def o_dev(col, k):
        return b_dev(1 - col, k)

    def a1_dev(col, k):
        b2 = plus(b_me[col], k // 2)
        return device(ctx, z, x_side(k), b2) if col == 0 else device(ctx, b2, x_side(k), y)

    def a1_slot(col, x2, b2):
        return col * 8 + (x2 * 4 + b2 if col == 0 else b2 * 2 + x2)

    def a1_at(col, x2, b2):
        return a1_0.at[x2, b2] if col == 0 else a1_1.at[b2, x2]

    def wt_at(k):
        return plus(z, k // 8), x_side(k), plus(y, k // 2)

    def wt_dev(k):
        return device(ctx, *wt_at(k))

    def x_at(k):
        return plus(x_me, k)

    def x_dev(k):
        x2 = x_at(k)
        return device((x2 // 2) * 2 + core, z, lax.rem(x2, 2), y)

    def rcopy(name, src, dst, slot_send, slot_recv, dev):
        return pltpu.make_async_remote_copy(
            src_ref=src, dst_ref=dst, send_sem=send_sem.at[BASE[name] + slot_send],
            recv_sem=recv_sem.at[BASE[name] + slot_recv], device_id=dev, device_id_type=MESH)

    started = []

    def send(name, src, dst, slot_send, slot_recv, dev):
        copy = rcopy(name, src, dst, slot_send, slot_recv, dev)
        copy.start()
        started.append(copy)
        return copy

    def sent(copies):
        for copy in copies:
            copy.wait_send()
        started[:] = [c for c in started if not any(c is copy for copy in copies)]

    def arrived(name, dst, slot):
        rcopy(name, dst, dst, 0, slot, partner).wait_recv()

    def lanes(i, width=128):
        return pl.ds(pl.multiple_of(i * width, width), width)

    load_kv = pltpu.make_async_copy(kvw_hbm, kv_src, load_sem.at[0])
    load_kv.start()
    for o2 in range(4):
        for x2 in range(2):
            for z2 in range(4):
                pltpu.make_async_copy(
                    wq_hbm.at[pl.ds(pl.multiple_of(128 + core * 64, 64), 64), pl.ds((z2 * 8 + x2 * 4 + o2) * 128, 128)],
                    w_src.at[o2 * 2 + x2, :, z2 * 128:(z2 + 1) * 128], load_sem.at[1]).start()
    first_rows = pl.ds(pl.multiple_of(core * 64, 64), 64)
    own_w = pltpu.make_async_copy(wq_hbm.at[first_rows, lanes(so_me[0], 512)], w1.at[0, so_me[0], core], load_sem.at[2])
    own_w.start()
    ctx_rows = pl.ds(pl.multiple_of(ctx * 1024, 1024), 1024)
    query_rows = pl.ds(pl.multiple_of(TOKENS + ctx * 256, 256), 256)
    tabs = [
        pltpu.make_async_copy(tabk_hbm.at[:, x_lo, y, :, ctx_rows], tab_kc, tab_sem.at[2]),
        pltpu.make_async_copy(tabk_hbm.at[:, x_lo, y, :, query_rows], tab_kq, tab_sem.at[3]),
        pltpu.make_async_copy(tabq_hbm.at[:, ctx_rows], tab_c, tab_sem.at[0]),
        pltpu.make_async_copy(tabq_hbm.at[:, query_rows], tab_q, tab_sem.at[1]),
    ]
    x_loads = [
        pltpu.make_async_copy(x_hbm.at[:, pl.ds(s * 1024, 1024)], x_v.at[s], x_sem.at[s])
        for s in range(NS)
    ]

    barrier = pltpu.get_barrier_semaphore()
    peers = [partner] + [x_dev(k) for k in range(1, 4)]
    peers += [wt_dev(k) for k in range(1, 32)]
    for col in range(2):
        peers += [so_dev(col, k) for k in (1, 3, 5, 7)]
    for dev in peers:
        pl.semaphore_signal(barrier, inc=1, device_id=dev, device_id_type=MESH)
    for copy in x_loads + tabs:
        copy.start()

    f = qx[...].astype(F32)
    for col in range(2):
        for bb in range(4):
            for t in range(4):
                at = [t * 2048 + bb * 256, t * 2048 + 1024 + bb * 256] if col == 0 else [
                    bb * 2048 + t * 256 + 128, bb * 2048 + 1024 + t * 256 + 128]
                tile = jnp.concatenate([f[:, c:c + 128] for c in at], axis=0)
                asend[col, bb, t * 16:(t + 1) * 16, :] = tile.astype(BF)
    a1_0[x_lo, y] = asend[0, y]
    a1_1[z, x_lo] = asend[1, z]

    core_cols = pl.ds(pl.multiple_of(core * 16, 16), 16)
    other_cols = pl.ds(pl.multiple_of(16 - core * 16, 16), 16)

    load_kv.wait()
    for g in range(4):
        for x2 in range(2):
            by_col = kv_src[:, g * 256 + x2 * 128:g * 256 + (x2 + 1) * 128].T
            if x2 == 0:
                by_col = jnp.concatenate(
                    [by_col[at + 16 * yy:at + 16 * yy + 16] for yy in range(4) for at in (0, 64)], axis=0)
            kvt[g, x2] = by_col.reshape(4, 32, 256)
    pltpu.make_async_copy(w_src, w_src, load_sem.at[1]).wait()
    w1[1, so_me[1], core] = w_src[so_me[1]]
    kva[0, :, core_cols, lanes(so_me[0])] = kvt[z, x_lo, :, core_cols, 0:128]
    for g in range(4):
        kva[1, g, core_cols, lanes(so_me[1])] = kvt[g, x_lo, y, core_cols, 128:256]
    kws[z, x_lo, y, core] = kvt[z, x_lo, y, :, lanes(core)]
    pl.semaphore_wait(barrier, len(peers))

    def kv_piece(col, k):
        o2 = plus(o_me[col], k // 2)
        if col == 0:
            return kvt.at[o2, x_side(k), :, core_cols, 0:128]
        return kvt.at[:, x_side(k), o2, core_cols, 128:256]

    half_lanes = lanes(core)
    for k in range(1, 32):
        z2, x2, y2 = wt_at(k)
        send("kvd", kvt.at[z2, x2, y2, :, half_lanes], kws.at[z, x_lo, y, core], k, wt, wt_dev(k))
    for k in (2, 6, 3, 7, 4, 5, 1):
        for col in range(2):
            send("a1", asend.at[col, plus(b_me[col], k // 2)], a1_at(col, x_lo, b_me[col]), col * 8 + k,
                 a1_slot(col, x_lo, b_me[col]), a1_dev(col, k))

    def w_piece(col, k):
        if col == 0:
            return wq_hbm.at[first_rows, lanes(so_at(0, k), 512)]
        return w_src.at[so_at(1, k)]

    def w2_at(col, so, b, c):
        o2, x2 = so // 2, lax.rem(so, 2)
        return w2.at[o2, x2, b, 0, c] if col == 0 else w2.at[b, x2, o2, 1, c]

    def w2_row(col, so, c):
        o2, x2 = so // 2, lax.rem(so, 2)
        return w2.at[o2, x2, :, 0, c] if col == 0 else w2.at[:, x2, o2, 1, c]

    def forward_w(col, k):
        so = so_at(col, k)
        if k > 0:
            arrived("w1", w1.at[col, so, core], col * 8 + so)
        for m in range(1, 4):
            send("w2", w1.at[col, so, core, :, lanes(plus(b_me[col], m))], w2_at(col, so, b_me[col], core),
                 (col * 8 + k) * 4 + m, (col * 8 + so) * 4 + b_me[col], b_dev(col, m))
        send("w1_p", w1.at[col, so, core], w1.at[col, so, core], col * 8 + k, col * 8 + so, partner)
        w2_at(col, so, b_me[col], core)[...] = w1[col, so, core, :, lanes(b_me[col])]

    for k in (2, 6, 3, 7, 1, 4, 5):
        for col in range(2):
            send("w1", w_piece(col, k), w1.at[col, so_me[col], core], col * 8 + k, col * 8 + so_me[col], so_dev(col, k))
    own_w.wait()
    for col in range(2):
        forward_w(col, 0)

    for col in range(2):
        for k in range(1, 8):
            x2, b2 = x_side(k), plus(b_me[col], k // 2)
            arrived("a1", a1_at(col, x2, b2), a1_slot(col, x2, b2))
    rows_at = (lambda o2: a_all.at[0, o2], lambda o2: a_all.at[1, :, :, o2])
    for k in (1, 3, 2):
        send("a2", a1_0, rows_at[0](z), k, z, o_dev(0, k))
        send("a2", a1_1, rows_at[1](y), 4 + k, 4 + y, o_dev(1, k))
    a_all[0, z] = a1_0[...]
    for z2 in range(4):
        for x2 in range(2):
            a_all[1, z2, x2, y] = a1_1[z2, x2]

    for k in (2, 6, 3, 7, 4, 5, 1):
        for col in range(2):
            send("kv1", kv_piece(col, k), kva.at[col, :, core_cols, lanes(so_me[col])], col * 8 + k, col * 8 + so_me[col], so_dev(col, k))

    near = (0, 1, 3, 2)
    order = (0, 2, 6, 3, 7, 1, 4, 5)
    for dz in near:
        z2 = plus(z, dz)
        for k in range(8 * dz, 8 * dz + 8):
            if k > 0:
                _, x2, y2 = wt_at(k)
                arrived("kvd", kws.at[z2, x2, y2, core], z2 * 8 + x2 * 4 + y2)
        send("kvd_p", kws.at[z2, :, :, core], kws.at[z2, :, :, core], dz, z2, partner)
    for copy in x_loads + tabs:
        copy.wait()
    u = None
    for dz in near:
        z2 = plus(z, dz)
        arrived("kvd_p", kws.at[z2, :, :, 1 - core], z2)
        for x2 in range(2):
            kw = jnp.concatenate([kws[z2, x2, yy, h] for yy in range(4) for h in range(2)], axis=1)
            part = nt_dot(kw, x_v[z2 * 2 + x2])
            u = part if u is None else u + part
        for k in {1: order[1:3], 3: order[3:5]}.get(dz, ()):
            for col in range(2):
                forward_w(col, k)
    low, high = u[0:16], u[16:32]
    cos, sin = tab_kc[0], tab_kc[1]
    kvc[x_hi, core, x_lo, y, 0:16, :] = (low * cos - high * sin).astype(BF)
    kvc[x_hi, core, x_lo, y, 16:32, :] = (high * cos + low * sin).astype(BF)

    own = kvc.at[x_hi, core, x_lo, y]
    for k in range(1, 4):
        send("kc_y", own, own, k, y, b_dev(0, k))
    for k in order[5:]:
        for col in range(2):
            forward_w(col, k)

    def turn_kc():
        for k in range(1, 4):
            arrived("kc_y", kvc.at[x_hi, core, x_lo, plus(y, k)], plus(y, k))
        row = kvc.at[x_hi, core, x_lo]
        for k in (2, 1, 3):
            send("kc_x", row, row, k, x_me, x_dev(k))
        send("kc_p", row, row, 0, x_me, partner)

    def share_kc():
        for k in (1, 3, 2):
            xs = x_at(k)
            row = kvc.at[xs // 2, core, lax.rem(xs, 2)]
            arrived("kc_x", row, xs)
            send("kc_p", row, row, k, xs, partner)

    def take_kc():
        for k in range(4):
            xs = x_at(k)
            arrived("kc_p", kvc.at[xs // 2, 1 - core, lax.rem(xs, 2)], xs)

    def prepare(c):
        for xh in range(2):
            kv = kvc[xh, c].reshape(8, 32, 1024)
            keys[xh * 2 + c] = jnp.concatenate(
                [kv[j, 0:16] for j in range(4)] + [kv[j, 16:32] for j in range(4)], axis=0)
            values[xh * 2 + c] = kv[4:8].reshape(128, 1024).T

    def turn_kq():
        for k in range(1, 4):
            arrived("kq_y", kvq.at[x_hi, core, x_lo, plus(y, k)], plus(y, k))
        row_y = kvq.at[x_hi, core, x_lo]
        for k in range(1, 4):
            send("kq_x", row_y, row_y, k, x_me, x_dev(k))

    def share_kq():
        for k in range(1, 4):
            xs = x_at(k)
            arrived("kq_x", kvq.at[xs // 2, core, lax.rem(xs, 2)], xs)
        send("kq_p", kvq.at[:, core], kvq.at[:, core], 0, 0, partner)

    def take_kq():
        arrived("kq_p", kvq.at[:, 1 - core], 0)

    def share_w(col, k):
        so = so_at(col, k)
        for m in range(1, 4):
            b2 = plus(b_me[col], m)
            arrived("w2", w2_at(col, so, b2, core), (col * 8 + so) * 4 + b2)
        send("w2_p", w2_row(col, so, core), w2_row(col, so, core), col * 8 + k, col * 8 + so, partner)

    for col in range(2):
        for k in range(1, 8):
            arrived("kv1", kva.at[col, :, core_cols, lanes(so_at(col, k))], col * 8 + so_at(col, k))
        send("kv1_p", kva.at[col, :, core_cols], kva.at[col, :, core_cols], col, col, partner)
    for col in range(2):
        arrived("kv1_p", kva.at[col, :, other_cols], col)
        for k in range(1, 4):
            o2 = plus(o_me[col], k)
            arrived("a2", rows_at[col](o2), col * 4 + o2)
        for t in range(4):
            v = a_all[col, :, :, :, t * 16:(t + 1) * 16, :].astype(F32).reshape(32, 2, 8, 128)
            ar[col, :, t * 256:t * 256 + 128] = v[:, 0].reshape(256, 128).astype(BF)
            ar[col, :, t * 256 + 128:(t + 1) * 256] = v[:, 1].reshape(256, 128).astype(BF)
        part = nt_dot(ar[col], kva[col].reshape(128, 1024)).T
        for bb in range(4):
            ck_send[col, bb] = part[bb * 32:(bb + 1) * 32, :]
        for k in range(1, 4):
            send("ck", ck_send.at[col, plus(b_me[col], k)], ck_recv.at[col, b_me[col]], col * 4 + k, col * 4 + b_me[col], b_dev(col, k))
        ck_recv[col, b_me[col]] = ck_send[col, b_me[col]]
    turn_kc()
    for col in range(2):
        for so in range(8):
            arrived("w1_p", w1.at[col, so, 1 - core], col * 8 + so)
        part = jnp.dot(ar[col], w1[col].reshape(1024, 512), preferred_element_type=F32)
        for bb in range(4):
            cq_send[col, bb] = part[:, bb * 128:(bb + 1) * 128]
        for k in range(1, 4):
            send("cq", cq_send.at[col, plus(b_me[col], k)], cq_recv.at[col, b_me[col]], col * 4 + k, col * 4 + b_me[col], b_dev(col, k))
        cq_recv[col, b_me[col]] = cq_send[col, b_me[col]]

    for col in range(2):
        for k in range(1, 4):
            b2 = plus(b_me[col], k)
            arrived("ck", ck_recv.at[col, b2], col * 4 + b2)
    u = ck_recv[0, 0]
    for i in range(1, 8):
        u = u + ck_recv[i // 4, i % 4]
    low, high = u[0:16], u[16:32]
    cos, sin = tab_kq[0], tab_kq[1]
    kvq[x_hi, core, x_lo, y, 0:16, :] = (low * cos - high * sin).astype(BF)
    kvq[x_hi, core, x_lo, y, 16:32, :] = (high * cos + low * sin).astype(BF)
    own_q = kvq.at[x_hi, core, x_lo, y]
    for k in range(1, 4):
        send("kq_y", own_q, own_q, k, y, b_dev(0, k))

    for k in order:
        for col in range(2):
            share_w(col, k)

    for col in range(2):
        for so in range(8):
            arrived("w2_p", w2_row(col, so, 1 - core), col * 8 + so)

    def heads(s):
        part = jnp.dot(x_v[s], w2[s // 2, s % 2].reshape(1024, D), preferred_element_type=F32)
        acc[...] = part if s == 0 else acc[...] + part

    for s in range(4):
        heads(s)
    turn_kq()
    for s in range(4, 8):
        heads(s)
    share_kc()

    @pl.loop(0, 4)
    def _(m):
        rows = pl.ds(pl.multiple_of(m * 256, 256), 256)
        u = acc[rows, :]
        acc[rows, :] = u * tab_c[0, rows, :] + pltpu.roll(u, 64, 1) * tab_c[1, rows, :]

    for col in range(2):
        for k in range(1, 4):
            b2 = plus(b_me[col], k)
            arrived("cq", cq_recv.at[col, b2], col * 4 + b2)
    u = cq_recv[0, 0]
    for i in range(1, 8):
        u = u + cq_recv[i // 4, i % 4]
    qq[...] = (u * tab_q[0] + pltpu.roll(u, 64, 1) * tab_q[1]).astype(BF)

    share_kq()
    prepare(core)
    take_kc()
    prepare(1 - core)

    for i in range(4):
        q = acc[i * 256:(i + 1) * 256, :].astype(BF)
        wide = (i + 1) * 256
        s_anchor = jnp.where(ctx > 0, scores_of(q, keys[0]), -1e30)
        s_own = scores_of(q, keys[ctx, :, 0:wide])
        row = lax.broadcasted_iota(jnp.int32, (256, wide), 0) + i * 256
        col = lax.broadcasted_iota(jnp.int32, (256, wide), 1)
        s_own = jnp.where(row >= col, s_own, -1e30)
        _, total, out = attend([s_anchor, s_own], [values[0], values[ctx, 0:wide, :]])
        c_out[i * 256:(i + 1) * 256, :] = (out / total).astype(BF)

    for i in range(2):
        rows = slice(i * 128, (i + 1) * 128)
        q = qq[rows, :]
        part_m[rows, :], part_l[rows, :], part_o[rows, :] = attend(
            [scores_of(q, keys[b]) for b in range(4)], [values[b] for b in range(4)])

    take_kq()
    for b in range(4):
        kv = kvq[b // 2, b % 2].reshape(8, 32, 256)
        qkeys[:, b * 256:(b + 1) * 256] = jnp.concatenate(
            [kv[j, 0:16] for j in range(4)] + [kv[j, 16:32] for j in range(4)], axis=0)
        qvalues[b * 256:(b + 1) * 256, :] = kv[4:8].reshape(128, 256).T
    for i in range(2):
        rows = slice(i * 128, (i + 1) * 128)
        s_self = scores_of(qq[rows, :], qkeys[...])
        row = lax.broadcasted_iota(jnp.int32, (128, 1024), 0) + (ctx * 256 + i * 128)
        col = lax.broadcasted_iota(jnp.int32, (128, 1024), 1)
        s_self = jnp.where(row >= col, s_self, -1e30)
        _, total, out = attend([s_self], [qvalues[...]], (part_m[rows, :], part_l[rows, :], part_o[rows, :]))
        q_out[rows, :] = (out / total).astype(BF)

    for copy in started:
        copy.wait_send()


def layer(context_x, query_x, w_query, key_value_weight, by_row, by_column):
    any_spec = pl.BlockSpec(memory_space=pl.ANY)
    vmem = pl.BlockSpec(memory_space=pltpu.VMEM)
    return pl.pallas_call(
        layer_kernel,
        out_shape=[jax.ShapeDtypeStruct((CTX_ROWS, D), BF), jax.ShapeDtypeStruct((Q_ROWS, D), BF)],
        in_specs=[any_spec, vmem, any_spec, any_spec, any_spec, any_spec],
        out_specs=[vmem, vmem],
        scratch_shapes=[
            pltpu.VMEM((NS, CTX_ROWS, 1024), BF),
            pltpu.VMEM((8, 64, 512), BF),
            pltpu.VMEM((256, 1024), BF),
            pltpu.VMEM((4, 2, 4, 32, 256), BF),
            pltpu.VMEM((2, 4, 32, 1024), BF),
            pltpu.VMEM((4, 2, 4, 2, 32, 128), BF),
            pltpu.VMEM((2, 8, 2, 64, 512), BF),
            pltpu.VMEM((4, 2, 4, 2, 2, 64, 128), BF),
            pltpu.VMEM((2, 4, 64, 128), BF),
            pltpu.VMEM((2, 4, 64, 128), BF),
            pltpu.VMEM((4, 2, 64, 128), BF),
            pltpu.VMEM((2, 4, 2, 4, 64, 128), BF),
            pltpu.VMEM((2, Q_ROWS, 1024), BF),
            pltpu.VMEM((2, 4, 32, Q_ROWS), F32),
            pltpu.VMEM((2, 4, 32, Q_ROWS), F32),
            pltpu.VMEM((2, 4, Q_ROWS, 128), F32),
            pltpu.VMEM((2, 4, Q_ROWS, 128), F32),
            pltpu.VMEM((2, 2, 2, 4, 32, 1024), BF),
            pltpu.VMEM((2, 2, 2, 4, 32, 256), BF),
            pltpu.VMEM((CTX_ROWS, D), F32),
            pltpu.VMEM((Q_ROWS, D), BF),
            pltpu.VMEM((4, 128, 1024), BF),
            pltpu.VMEM((4, 1024, 128), BF),
            pltpu.VMEM((128, 1024), BF),
            pltpu.VMEM((1024, 128), BF),
            pltpu.VMEM((Q_ROWS, 1), F32),
            pltpu.VMEM((Q_ROWS, 1), F32),
            pltpu.VMEM((Q_ROWS, D), F32),
            pltpu.VMEM((2, CTX_ROWS, D), F32),
            pltpu.VMEM((2, Q_ROWS, D), F32),
            pltpu.VMEM((2, 16, 1024), F32),
            pltpu.VMEM((2, 16, 256), F32),
            pltpu.SemaphoreType.DMA((SLOTS,)),
            pltpu.SemaphoreType.DMA((SLOTS,)),
            pltpu.SemaphoreType.DMA((NS,)),
            pltpu.SemaphoreType.DMA((4,)),
            pltpu.SemaphoreType.DMA((3,)),
        ],
        compiler_params=pltpu.CompilerParams(
            collective_id=0, has_side_effects=True, vmem_limit_bytes=VMEM_LIMIT),
        name="layer",
    )(context_x, query_x, w_query, key_value_weight, by_row, by_column)


def finish_kernel(c_from, q_from, c_to, q_to):
    c_to[...] = c_from[...]
    q_to[...] = q_from[...]


def finish(c, q):
    return pl.pallas_call(
        finish_kernel,
        out_shape=[jax.ShapeDtypeStruct(c.shape, BF), jax.ShapeDtypeStruct(q.shape, BF)],
        name="finish",
    )(c, q)


def per_device(context_x, query_x, w_query, key_value_weight):
    by_row, by_column = rope_tables()
    return tuple(finish(*layer(
        context_x, query_x, w_query, key_value_weight, jnp.asarray(by_row), jnp.asarray(by_column))))


def solution(mesh):
    placed = (P("ctx", None), P(("ctx", "wt"), None), P("wt", None), P("wt", None))
    return jax.shard_map(
        per_device,
        mesh=mesh,
        in_specs=placed,
        out_specs=(P("ctx", "wt"), P("ctx", "wt")),
        check_vma=False,
    )
```

time: 648 us -> 68.5 us (0.11)
  waiting for transfers between devices: 520 us -> 0 us
  Pallas kernels: 0 us -> 67.7 us
  matrix products: 58.4 us -> 0 us
  local copies, waits for them, and re-layouts: 16.5 us -> 0 us
  other arithmetic: 14.9 us -> 0 us
  between operations: 14 us -> 0.64 us
  blocking collectives: 13.2 us -> 0 us
  starting transfers between devices: 10.2 us -> 0 us
    all_gather x3 -> x0, waiting for transfers between devices: 470 us -> none  [the longest x1 316 us: per_device(): piece = lax.all_gather(query_x, ('ctx', 'wt'), axis=0, tiled=True)]
    pallas_call x0 -> x2, Pallas kernels: none -> 67.7 us  [the longest x1 66 us: layer(): pl.pallas_call(layer_kernel, out_shape=[jax.ShapeDtypeStruct((CTX_ROWS, D...]
    dot_general x12 -> x0, matrix products: 58.4 us -> none  [the longest x1 12.6 us: per_device(): jnp.dot(context_x, pair_cols, preferred_element_type=jnp.float32)]
    all_to_all x1 -> x0, waiting for transfers between devices: 48.5 us -> none  [per_device(): lax.all_to_all(w_query, 'wt', split_axis=1, concat_axis=0, tiled=True)]
    all_gather x2 -> x0, blocking collectives: 13.2 us -> none  [joined(): gathered = jax.tree.map(lambda a: lax.all_gather(a, axis), part)]
    all_to_all x1 -> x0, starting transfers between devices: 9.81 us -> none  [per_device(): lax.all_to_all(w_query, 'wt', split_axis=1, concat_axis=0, tiled=True)]
    unnamed x14 -> x0, local copies, waits for them, and re-layouts: 8.22 us -> none
  transfers between devices with their start and end apart: 5 -> 0, of which waited for: 4 -> 0; matrix products, arithmetic and copies ran while one was open for 12% -> 0% of each run, Pallas kernels for 0% -> 0%
where the time goes in v2:
time: 68.5 us; the launch traced here: 68.3 us
  Pallas kernels  67.7 us (99%)
    pallas_call x1, Pallas kernels, layer(): pl.pallas_call(layer_kernel, out_shape=[jax.ShapeDtypeStruct((CTX_ROWS, D...  66 us
    pallas_call x1, Pallas kernels, finish(): pl.pallas_call(finish_kernel, out_shape=[jax.ShapeDtypeStruct(c.shape, BF...  1.69 us

profile of v2, /device:TPU:1, one launch (start us, length us, event | category | flops | bytes accessed | tf_op | source)
XLA Modules:
  0.0 68.3 jit_solution(15244294681435904541)
XLA Ops:
  0.6 66.0 %layer.1 = (bf16[1024,128]{1,0:T(8,128)(2,1)}, bf16[256,128]{1,0:T(8,128)(2,1)}) custom-call(bf16[1024,8192]{1,0:T(8,128)(2,1)} %x_hbm.1, bf16[8,8192]{1,0:T(8,128)(2,1)} %qx.1, bf16[256,4096]{1,0:T(8,128)(2,1)} %wq_hbm.1, bf16[256,1024]{1,0:T(8,128)(2,1)} %kvw_hbm.1, f32[2,5120,128]{2,1,0:T(8,128)} %constant.4.clone.tabq_hbm, ...), custom_call_target="tpu_custom_call" | custom-call | tf_op jit(solution)/shard_map/layer/pallas_call | solution.py:490
  66.6 1.7 %finish.1 = (bf16[1024,128]{1,0:T(8,128)(2,1)}, bf16[256,128]{1,0:T(8,128)(2,1)}) custom-call(bf16[1024,128]{1,0:T(8,128)(2,1)} %get-tuple-element.4.c_from, bf16[256,128]{1,0:T(8,128)(2,1)} %get-tuple-element.5.q_from), custom_call_target="tpu_custom_call" | custom-call | tf_op jit(solution)/shard_map/finish/pallas_call | solution.py:546

commit v3 on v2

--- a/solution.py
+++ b/solution.py
@@ -299,9 +299,6 @@
             kw = jnp.concatenate([kws[z2, x2, yy, h] for yy in range(4) for h in range(2)], axis=1)
             part = nt_dot(kw, x_v[z2 * 2 + x2])
             u = part if u is None else u + part
-        for k in {1: order[1:3], 3: order[3:5]}.get(dz, ()):
-            for col in range(2):
-                forward_w(col, k)
     low, high = u[0:16], u[16:32]
     cos, sin = tab_kc[0], tab_kc[1]
     kvc[x_hi, core, x_lo, y, 0:16, :] = (low * cos - high * sin).astype(BF)
@@ -310,7 +307,7 @@
     own = kvc.at[x_hi, core, x_lo, y]
     for k in range(1, 4):
         send("kc_y", own, own, k, y, b_dev(0, k))
-    for k in order[5:]:
+    for k in order[1:]:
         for col in range(2):
             forward_w(col, k)
 
@@ -363,6 +360,8 @@
             b2 = plus(b_me[col], m)
             arrived("w2", w2_at(col, so, b2, core), (col * 8 + so) * 4 + b2)
         send("w2_p", w2_row(col, so, core), w2_row(col, so, core), col * 8 + k, col * 8 + so, partner)
+
+    turn_kc()
 
     for col in range(2):
         for k in range(1, 8):
@@ -383,7 +382,6 @@
         for k in range(1, 4):
             send("ck", ck_send.at[col, plus(b_me[col], k)], ck_recv.at[col, b_me[col]], col * 4 + k, col * 4 + b_me[col], b_dev(col, k))
         ck_recv[col, b_me[col]] = ck_send[col, b_me[col]]
-    turn_kc()
     for col in range(2):
         for so in range(8):
             arrived("w1_p", w1.at[col, so, 1 - core], col * 8 + so)
@@ -424,9 +422,9 @@
     for s in range(4):
         heads(s)
     turn_kq()
+    share_kc()
     for s in range(4, 8):
         heads(s)
-    share_kc()
 
     @pl.loop(0, 4)
     def _(m):
@@ -434,21 +432,13 @@
         u = acc[rows, :]
         acc[rows, :] = u * tab_c[0, rows, :] + pltpu.roll(u, 64, 1) * tab_c[1, rows, :]
 
-    for col in range(2):
-        for k in range(1, 4):
-            b2 = plus(b_me[col], k)
-            arrived("cq", cq_recv.at[col, b2], col * 4 + b2)
-    u = cq_recv[0, 0]
-    for i in range(1, 8):
-        u = u + cq_recv[i // 4, i % 4]
-    qq[...] = (u * tab_q[0] + pltpu.roll(u, 64, 1) * tab_q[1]).astype(BF)
-
-    share_kq()
     prepare(core)
     take_kc()
     prepare(1 - core)
 
     for i in range(4):
+        if i == 2:
+            share_kq()
         q = acc[i * 256:(i + 1) * 256, :].astype(BF)
         wide = (i + 1) * 256
         s_anchor = jnp.where(ctx > 0, scores_of(q, keys[0]), -1e30)
@@ -458,6 +448,15 @@
         s_own = jnp.where(row >= col, s_own, -1e30)
         _, total, out = attend([s_anchor, s_own], [values[0], values[ctx, 0:wide, :]])
         c_out[i * 256:(i + 1) * 256, :] = (out / total).astype(BF)
+
+    for col in range(2):
+        for k in range(1, 4):
+            b2 = plus(b_me[col], k)
+            arrived("cq", cq_recv.at[col, b2], col * 4 + b2)
+    u = cq_recv[0, 0]
+    for i in range(1, 8):
+        u = u + cq_recv[i // 4, i % 4]
+    qq[...] = (u * tab_q[0] + pltpu.roll(u, 64, 1) * tab_q[1]).astype(BF)
 
     for i in range(2):
         rows = slice(i * 128, (i + 1) * 128)

time: 68.5 us -> 67.4 us (0.984)
  Pallas kernels: 67.7 us -> 66.6 us
    pallas_call x1, Pallas kernels: 66 us -> 64.9 us  [layer(): pl.pallas_call(layer_kernel, out_shape=[jax.ShapeDtypeStruct((CTX_ROWS, D...]
where the time goes in v3:
time: 67.4 us; the launch traced here: 67.3 us
  Pallas kernels  66.6 us (99%)
    pallas_call x1, Pallas kernels, layer(): pl.pallas_call(layer_kernel, out_shape=[jax.ShapeDtypeStruct((CTX_ROWS, D...  64.9 us
    pallas_call x1, Pallas kernels, finish(): pl.pallas_call(finish_kernel, out_shape=[jax.ShapeDtypeStruct(c.shape, BF...  1.69 us

profile of v3, /device:TPU:1, one launch (start us, length us, event | category | flops | bytes accessed | tf_op | source)
XLA Modules:
  0.0 67.3 jit_solution(5920908715960053365)
XLA Ops:
  0.6 64.9 %layer.1 = (bf16[1024,128]{1,0:T(8,128)(2,1)}, bf16[256,128]{1,0:T(8,128)(2,1)}) custom-call(bf16[1024,8192]{1,0:T(8,128)(2,1)} %x_hbm.1, bf16[8,8192]{1,0:T(8,128)(2,1)} %qx.1, bf16[256,4096]{1,0:T(8,128)(2,1)} %wq_hbm.1, bf16[256,1024]{1,0:T(8,128)(2,1)} %kvw_hbm.1, f32[2,5120,128]{2,1,0:T(8,128)} %constant.4.clone.tabq_hbm, ...), custom_call_target="tpu_custom_call" | custom-call | tf_op jit(solution)/shard_map/layer/pallas_call | solution.py:489
  65.6 1.7 %finish.1 = (bf16[1024,128]{1,0:T(8,128)(2,1)}, bf16[256,128]{1,0:T(8,128)(2,1)}) custom-call(bf16[1024,128]{1,0:T(8,128)(2,1)} %get-tuple-element.4.c_from, bf16[256,128]{1,0:T(8,128)(2,1)} %get-tuple-element.5.q_from), custom_call_target="tpu_custom_call" | custom-call | tf_op jit(solution)/shard_map/finish/pallas_call | solution.py:545
